TPU v7x, 32 devices: a whole 2x2x4 slice. The times are simulated.
32 devices in a mesh: tiles: 16 (over z, x, core), dp: 2 (over y).
Axes of the slice: x: 2, y: 2, z: 4, core: 2. Of those that a mesh axis runs over, the one named last changes fastest.
Arguments:
- fields: bfloat16 [2, 48, 16, 16, 256], P('dp', 'tiles'), may hold values from -6 to 6
- grad_out: bfloat16 [2, 48, 16, 16, 256], P('dp', 'tiles'), may hold values from -6 to 6
- block_count: int32 [16], P('tiles'), may hold values from 1 to 3, as said below
- ocean: int32 [48], P('tiles'), may hold values from 0 to 1, as said below
- kernel: bfloat16 [7, 7, 256], replicated, may hold values from -0.875 to 0.875
- ln_gain: float32 [256], replicated, may hold values from 0.1 to 1.9
- w_in: bfloat16 [256, 1024], replicated, may hold values from -0.375 to 0.375
- w_out: bfloat16 [1024, 256], replicated, may hold values from -0.1875 to 0.1875
- layer_scale: float32 [256], replicated, may hold values from 0.3 to 1.5
Outputs:
- state_next: bfloat16 [2, 48, 16, 16, 256], P('dp', 'tiles')
- grad_fields: bfloat16 [2, 48, 16, 16, 256], P('dp', 'tiles')
- grad_kernel: float32 [7, 7, 256], replicated
- grad_gain: float32 [256], replicated
- grad_w_in: float32 [256, 1024], replicated
- grad_w_out: float32 [1024, 256], replicated
- grad_scale: float32 [256], replicated
Inputs may be any that keep to these rules, and one draw needn't show every extreme that they name: Index i of tiles owns block_count[i] consecutive cycle tiles in its first slots, in the cycle order of the first step; index i and index i + H (i < H, H half the number of entries) own equally many; some index owns 3 and some index owns one. 1 marks an ocean tile; the first and the last cycle tile that each index of tiles owns are ocean.
All inputs are finite; a program needn't handle non-finite values.
Results may differ from a plain program's by a relative error of at most 0.0066.
Values may be sent and summed in bfloat16 or wider, within the bound.
No kernel may reach another device: no remote copies, remote signals or barrier semaphores. Data moves between devices by JAX's collectives and lax.ppermute only.
A program may use at most 64 MiB of HBM per device.

v0:
```python
import jax
import jax.numpy as jnp
from jax import lax
from jax.sharding import PartitionSpec as P

HID = 1024
KSIZE = 7


EPS = 1e-06


def passed_along(block, axis, distance):
    devices = range(lax.axis_size(axis))
    route = [(i - distance, i) for i in devices if i - distance in devices]
    return lax.ppermute(block, axis, route)


def from_partner(block, axis, distance):
    count = lax.axis_size(axis)
    route = []
    for low in range(count):
        high = low | 1 << distance
        if high != low and high < count:
            route += [(low, high), (high, low)]
    return lax.ppermute(block, axis, route)


def gelu_tanh(inputs):
    return jax.nn.gelu(inputs, approximate=True)


def depthwise(padded, kernel_f, tile_rows, tile_cols):
    running = jnp.zeros(padded.shape[:-3] + (tile_rows, tile_cols, padded.shape[-1]), jnp.float32)
    for row_shift in range(KSIZE):
        for col_shift in range(KSIZE):
            window = padded[
                ..., row_shift : row_shift + tile_rows, col_shift : col_shift + tile_cols, :
            ]
            running = running + kernel_f[row_shift, col_shift] * window.astype(jnp.float32)
    return running


def kernel_terms(conv_grad, padded, tile_rows, tile_cols):
    grad_f = conv_grad.astype(jnp.float32)
    leading = tuple(range(grad_f.ndim - 1))
    stacked = []
    for row_shift in range(KSIZE):
        taps = []
        for col_shift in range(KSIZE):
            window = padded[
                ..., row_shift : row_shift + tile_rows, col_shift : col_shift + tile_cols, :
            ]
            taps.append(jnp.sum(grad_f * window.astype(jnp.float32), axis=leading))
        stacked.append(jnp.stack(taps))
    return jnp.stack(stacked)


def spread(conv_grad, kernel_f, tile_rows, tile_cols):
    reach = KSIZE - 1
    widths = [(0, 0)] * (conv_grad.ndim - 3) + [(reach, reach), (reach, reach), (0, 0)]
    grad_f = jnp.pad(conv_grad.astype(jnp.float32), widths)
    running = jnp.zeros(
        conv_grad.shape[:-3] + (tile_rows + reach, tile_cols + reach, conv_grad.shape[-1]),
        jnp.float32,
    )
    for row_shift in range(KSIZE):
        for col_shift in range(KSIZE):
            window = grad_f[
                ...,
                reach - row_shift : reach - row_shift + tile_rows + reach,
                reach - col_shift : reach - col_shift + tile_cols + reach,
                :,
            ]
            running = running + kernel_f[row_shift, col_shift] * window
    return running


def make_block(ln_gain, w_in, w_out, layer_scale):

    def block_step(totals, inputs):
        convolved, skip_rows, cell_mask, tangent = inputs
        row_mean = jnp.mean(convolved, axis=-1, keepdims=True)
        centred = convolved - row_mean
        variance = jnp.mean(centred * centred, axis=-1, keepdims=True)
        inverse = lax.rsqrt(variance + EPS)
        yhat = centred * inverse
        normed = (yhat * ln_gain).astype(jnp.bfloat16)
        preact = jnp.dot(normed, w_in, preferred_element_type=jnp.float32)
        activated = gelu_tanh(preact).astype(jnp.bfloat16)
        projected = jnp.dot(activated, w_out, preferred_element_type=jnp.float32)
        tangent_f = tangent.astype(jnp.float32)
        state = (cell_mask * (skip_rows.astype(jnp.float32) + layer_scale * projected)).astype(
            jnp.bfloat16
        )
        dproj = (cell_mask * layer_scale * tangent_f).astype(jnp.bfloat16)
        scale_part = jnp.sum(cell_mask * tangent_f * projected, axis=0)
        w_out_part = lax.dot_general(
            activated, dproj, (((0,), (0,)), ((), ())), preferred_element_type=jnp.float32
        )
        dactivated = lax.dot_general(
            dproj, w_out, (((1,), (1,)), ((), ())), preferred_element_type=jnp.float32
        )
        unused, pullback = jax.vjp(gelu_tanh, preact)
        dpreact = pullback(dactivated)[0].astype(jnp.bfloat16)
        w_in_part = lax.dot_general(
            normed, dpreact, (((0,), (0,)), ((), ())), preferred_element_type=jnp.float32
        )
        dnormed = lax.dot_general(
            dpreact, w_in, (((1,), (1,)), ((), ())), preferred_element_type=jnp.float32
        )
        gain_part = jnp.sum(dnormed * yhat, axis=0)
        dhat = dnormed * ln_gain
        conv_grad = inverse * (
            dhat
            - jnp.mean(dhat, axis=-1, keepdims=True)
            - yhat * jnp.mean(dhat * yhat, axis=-1, keepdims=True)
        )
        totals = (gain_part, w_in_part, w_out_part, scale_part)
        return (totals, (state, conv_grad.astype(jnp.bfloat16)))

    return block_step


def shards(fields, grad_out, block_count, ocean, kernel, ln_gain, w_in, w_out, layer_scale):
    samples, slot_count, tile_rows, tile_cols, channels = fields.shape
    half_kernel = KSIZE // 2
    half_axis = lax.axis_size("tiles") // 2
    top_bit = lax.axis_size("tiles").bit_length() - 2
    here = lax.axis_index("tiles")
    lower_half = here < half_axis
    at_start = here % half_axis == 0
    at_end = here % half_axis == half_axis - 1
    owned = block_count[0]
    strip_width = slot_count * tile_cols
    used_cols = owned * tile_cols
    slot_ids = jnp.arange(slot_count, dtype=jnp.int32)
    slot_mask = jnp.logical_and(slot_ids < owned, ocean > 0).astype(jnp.float32)
    masked = fields * slot_mask.astype(jnp.bfloat16)[None, :, None, None, None]
    strip = jnp.transpose(masked, (0, 2, 1, 3, 4)).reshape(
        samples, tile_rows, strip_width, channels
    )
    tangent = jnp.transpose(grad_out, (0, 2, 1, 3, 4)).reshape(
        samples, tile_rows, strip_width, channels
    )
    mask_strip = jnp.broadcast_to(
        slot_mask[None, None, :, None, None], (samples, tile_rows, slot_count, tile_cols, 1)
    ).reshape(samples, tile_rows, strip_width, 1)
    left_edge = strip[:, :, :half_kernel]
    right_edge = lax.dynamic_slice_in_dim(strip, used_cols - half_kernel, half_kernel, 2)
    up_send = jnp.where(lower_half, right_edge, left_edge)
    down_send = jnp.where(lower_half, left_edge, right_edge)
    from_lower = passed_along(up_send, "tiles", 1)
    from_upper = passed_along(down_send, "tiles", -1)
    far_edges = from_partner(jnp.stack([down_send, up_send]), "tiles", top_bit)
    from_lower = jnp.where(at_start, far_edges[0], from_lower)
    from_upper = jnp.where(at_end, far_edges[1], from_upper)
    from_west = jnp.where(lower_half, from_lower, from_upper)
    from_east = jnp.where(lower_half, from_upper, from_lower)
    blank_cols = jnp.zeros((samples, tile_rows, half_kernel, channels), jnp.bfloat16)
    extended = jnp.concatenate([from_west, strip, blank_cols], axis=2)
    extended = lax.dynamic_update_slice_in_dim(extended, from_east, used_cols + half_kernel, 2)
    mirrored = from_partner(extended[:, tile_rows - half_kernel :], "tiles", top_bit)
    north_rows = jnp.roll(mirrored[:, ::-1, ::-1], used_cols - strip_width, axis=2)
    south_rows = jnp.zeros(
        (samples, half_kernel, strip_width + 2 * half_kernel, channels), jnp.bfloat16
    )
    padded = jnp.concatenate([south_rows, extended, north_rows], axis=1)
    kernel_f = kernel.astype(jnp.float32)
    convolved = depthwise(padded, kernel_f, tile_rows, strip_width)
    block_step = make_block(ln_gain, w_in, w_out, layer_scale)
    start_totals = (
        jnp.zeros((channels,), jnp.float32),
        jnp.zeros((channels, HID), jnp.float32),
        jnp.zeros((HID, channels), jnp.float32),
        jnp.zeros((channels,), jnp.float32),
    )
    totals, outputs = block_step(
        start_totals,
        (
            convolved.reshape(-1, channels),
            strip.reshape(-1, channels),
            mask_strip.reshape(-1, 1),
            tangent.reshape(-1, channels),
        ),
    )
    gain_part, w_in_part, w_out_part, scale_part = totals
    conv_grad = outputs[1].reshape(samples, tile_rows, strip_width, channels)
    kernel_part = kernel_terms(conv_grad, padded, tile_rows, strip_width)
    dpadded = spread(conv_grad, kernel_f, tile_rows, strip_width)
    north_grad = dpadded[:, tile_rows + half_kernel :]
    returned = from_partner(
        jnp.roll(north_grad[:, ::-1, ::-1], used_cols - strip_width, axis=2).astype(jnp.bfloat16),
        "tiles",
        top_bit,
    ).astype(jnp.float32)
    dextended = dpadded[:, half_kernel : tile_rows + half_kernel]
    dextended = dextended.at[:, tile_rows - half_kernel :].add(returned)
    west_grad = dextended[:, :, :half_kernel]
    east_grad = lax.dynamic_slice_in_dim(dextended, used_cols + half_kernel, half_kernel, 2)
    core_grad = dextended[:, :, half_kernel : strip_width + half_kernel]
    up_grad = jnp.where(lower_half, east_grad, west_grad)
    down_grad = jnp.where(lower_half, west_grad, east_grad)
    grad_lower = passed_along(up_grad.astype(jnp.bfloat16), "tiles", 1).astype(up_grad.dtype)
    grad_upper = passed_along(down_grad.astype(jnp.bfloat16), "tiles", -1).astype(down_grad.dtype)
    far_grads = from_partner(
        jnp.stack([down_grad, up_grad]).astype(jnp.bfloat16), "tiles", top_bit
    ).astype(jnp.float32)
    grad_lower = jnp.where(at_start, far_grads[0], grad_lower)
    grad_upper = jnp.where(at_end, far_grads[1], grad_upper)
    to_head = jnp.where(lower_half, grad_lower, grad_upper)
    to_tail = jnp.where(lower_half, grad_upper, grad_lower)
    core_grad = core_grad.at[:, :, :half_kernel].add(to_head)
    tail_cols = (
        lax.dynamic_slice_in_dim(core_grad, used_cols - half_kernel, half_kernel, 2) + to_tail
    )
    core_grad = lax.dynamic_update_slice_in_dim(core_grad, tail_cols, used_cols - half_kernel, 2)
    grad_strip = (mask_strip * (tangent.astype(jnp.float32) + core_grad)).astype(jnp.bfloat16)
    kernel_sum, gain_sum, w_in_sum, w_out_sum, scale_sum = lax.psum(
        (kernel_part, gain_part, w_in_part, w_out_part, scale_part), ("tiles", "dp")
    )
    norm = (
        samples * lax.axis_size("dp") * slot_count * lax.axis_size("tiles") * tile_rows * tile_cols
    ) ** (-0.5)
    state_next = jnp.transpose(
        outputs[0].reshape(samples, tile_rows, slot_count, tile_cols, channels), (0, 2, 1, 3, 4)
    )
    grad_fields = jnp.transpose(
        grad_strip.reshape(samples, tile_rows, slot_count, tile_cols, channels), (0, 2, 1, 3, 4)
    )
    return (
        state_next,
        grad_fields,
        kernel_sum * norm,
        gain_sum * norm,
        w_in_sum * norm,
        w_out_sum * norm,
        scale_sum * norm,
    )


def solution(mesh):
    placed = (
        P("dp", "tiles", None, None, None),
        P("dp", "tiles", None, None, None),
        P("tiles"),
        P("tiles"),
        P(),
        P(),
        P(),
        P(),
        P(),
    )
    return jax.shard_map(
        shards,
        mesh=mesh,
        in_specs=placed,
        out_specs=(
            P("dp", "tiles", None, None, None),
            P("dp", "tiles", None, None, None),
            P(),
            P(),
            P(),
            P(),
            P(),
        ),
        check_vma=False,
    )
```

profile of v0, /device:TPU:0, one launch (start us, length us, event | category | flops | bytes accessed | tf_op | source)
XLA Modules:
  0.0 257.7 jit_solution(4455528397597867522)
XLA Ops:
  7.9 0.7 fusion.239
  8.6 1.1 copy_multiply_fusion
  9.7 2.4 collective-permute-start.1
  12.1 1.3 collective-permute-start.2
  13.5 6.9 %collective-permute-start = (bf16[2,1,16,3,256]{4,3,2,1,0:T(4,128)(2,1)S(1)}, bf16[2,1,16,3,256]{4,3,2,1,0:T(4,128)(2,1)S(1)}, u32[]{:S(2)}, u32[]{:S(2)}) collective-permute-start(bf16[2,1,16,3,256]{4,3,2,1,0:T(4,128)(2,1)S(1)} %pad_maximum_fusion.1), channel_id=1, source_target_pairs={{0,16},{16,0},{2,18},{18,2},{4,20},{20,4},{6,22},{22,6},{8,24},{24... | collective-permute-start | bytes 147464 | tf_op jit(solution)/shard_map/ppermute | solution.py:26
  20.4 1.0 fusion.240
  21.4 1.0 fusion.241
  22.6 0.4 collective-permute-done
  23.1 0.3 maximum_maximum_fusion
  23.4 0.2 dynamic_update_slice.6
  23.6 2.6 %collective-permute-start.3 = (bf16[1,3,54,256]{3,2,1,0:T(8,128)(2,1)S(1)}, bf16[1,3,54,256]{3,2,1,0:T(8,128)(2,1)S(1)}, u32[]{:S(2)}, u32[]{:S(2)}) collective-permute-start(bf16[1,3,54,256]{3,2,1,0:T(8,128)(2,1)S(1)} %slice.869), channel_id=1, source_target_pairs={{0,16},{16,0},{2,18},{18,2},{4,20},{20,4},{6,22},{22,6},{8,24},{24... | collective-permute-start | bytes 248840 | tf_op jit(solution)/shard_map/ppermute | solution.py:26
  26.2 1.0 fusion.242
  27.6 0.6 broadcast_in_dim.14
  28.2 0.9 collective-permute-done.3
  29.3 8.2 %fusion.237 = (f32[16,48]{1,0:T(8,128)S(1)}, f32[1,16,48,256]{3,2,1,0:T(8,128)S(1)}) fusion(bf16[1,3,54,256]{3,2,1,0:T(8,128)(2,1)S(1)} %fusion.232, bf16[1,16,54,256]{3,2,1,0:T(8,128)(2,1)S(1)} %dynamic_update_slice.6, f32[256]{0:T(256)S(1)} %bitcast.319, f32[256]{0:T(256)S(1)} %bitcast.317, f32[256]{0:T(256)S(1)} %bitcast.315, f32[256]{0:T(256)S(1)} %bitcast.313, ...), kind=kLoop, calls=%fused_computation.458 | loop fusion | flops 41286912 | bytes 4136960 | tf_op jit(solution)/shard_map/reduce_sum | solution.py:83
  37.8 0.3 multiply_reduce_fusion.2
  38.2 0.3 multiply_convert_fusion.2
  38.5 1.2 multiply_convert_fusion
  39.7 2.0 fusion.207
  41.8 1.6 fusion.244
  43.4 2.4 fusion.6
  45.8 1.6 fusion.243
  47.4 2.1 multiply_reduce_fusion
  49.5 0.5 multiply_convert_fusion.1
  50.0 1.6 fusion.198
  51.6 1.2 fusion.199
  52.8 1.2 fusion.200
  54.0 1.9 fusion.179
  56.6 40.4 %all-reduce.2 = (f32[7,7,256]{2,1,0:T(8,128)S(1)}, f32[256]{0:T(256)S(1)}, f32[256]{0:T(256)S(1)}) all-reduce(f32[7,7,256]{2,1,0:T(8,128)S(1)} %constant_dynamic-update-slice_fusion, f32[256]{0:T(256)S(1)} %copy-done.49, f32[256]{0:T(256)S(1)} %copy-done.48), channel_id=1, replica_groups=mesh['tiles'=16,'dp'=2] {'tiles','dp'}, use_global_device_ids=true, to_apply=%region_53.54 | all-reduce | flops 13056 | bytes 104448 | tf_op jit(solution)/shard_map/psum | solution.py:219
  97.0 0.6 broadcast_multiply_fusion.2
  97.8 10.0 %fusion.100 = f32[1,22,54,256]{3,2,1,0:T(8,128)S(1)} fusion(f32[1,16,48,256]{3,2,1,0:T(8,128)S(1)} %convert.16, f32[256]{0:T(256)S(1)} %bitcast.320, f32[256]{0:T(256)S(1)} %bitcast.318, f32[256]{0:T(256)S(1)} %bitcast.316, f32[256]{0:T(256)S(1)} %bitcast.314, f32[256]{0:T(256)S(1)} %bitcast.312, f32[256]{0:T(256)S(1)} %bitcast.310, f32[256]{0:T(256)S(1)} %bitcast.308, ...), kind=kLoop, calls=%fused_computation.221 | loop fusion | flops 29500416 | bytes 2053120 | tf_op jit(solution)/shard_map/add | solution.py:75
  107.9 0.2 rev.7
  108.1 3.0 %collective-permute-start.4 = (bf16[1,3,54,256]{3,2,1,0:T(8,128)(2,1)S(1)}, bf16[1,3,54,256]{3,2,1,0:T(8,128)(2,1)S(1)}, u32[]{:S(2)}, u32[]{:S(2)}) collective-permute-start(bf16[1,3,54,256]{3,2,1,0:T(8,128)(2,1)S(1)} %fusion.230), channel_id=1, source_target_pairs={{0,16},{16,0},{2,18},{18,2},{4,20},{20,4},{6,22},{22,6},{8,24},{24... | collective-permute-start | bytes 248840 | tf_op jit(solution)/shard_map/ppermute | solution.py:26
  111.1 0.6 broadcast_multiply_fusion.6
  111.8 2.3 collective-permute-done.4
  114.2 1.3 collective-permute-start.6
  115.5 1.3 collective-permute-start.7
  116.8 6.4 %collective-permute-start.5 = (bf16[2,1,16,3,256]{4,3,2,1,0:T(4,128)(2,1)S(1)}, bf16[2,1,16,3,256]{4,3,2,1,0:T(4,128)(2,1)S(1)}, u32[]{:S(2)}, u32[]{:S(2)}) collective-permute-start(bf16[2,1,16,3,256]{4,3,2,1,0:T(4,128)(2,1)S(1)} %pad_maximum_fusion.2), channel_id=1, source_target_pairs={{0,16},{16,0},{2,18},{18,2},{4,20},{20,4},{6,22},{22,6},{8,24},{24... | collective-permute-start | bytes 147464 | tf_op jit(solution)/shard_map/ppermute | solution.py:26
  123.2 0.6 broadcast_multiply_fusion.7
  123.8 0.8 copy.28
  124.6 4.6 %collective-permute-done.5 = bf16[2,1,16,3,256]{4,3,2,1,0:T(4,128)(2,1)S(1)} collective-permute-done((bf16[2,1,16,3,256]{4,3,2,1,0:T(4,128)(2,1)S(1)}, bf16[2,1,16,3,256]{4,3,2,1,0:T(4,128)(2,1)S(1)}, u32[]{:S(2)}, u32[]{:S(2)}) %collective-permute-start.5) | collective-permute-done | bytes 49184 | tf_op jit(solution)/shard_map/ppermute | solution.py:26
  129.3 0.3 scatter-add.9
  129.7 0.3 dynamic_update_slice.7
  129.9 0.2 fusion.202
  130.1 0.8 copy.22
  130.9 116.5 %all-reduce.6.cloned.1.call-done = (f32[256,1024]{1,0:T(8,128)}, f32[1024,256]{1,0:T(8,128)}) async-done(((f32[256,1024]{1,0:T(8,128)}, f32[1024,256]{1,0:T(8,128)}), (f32[256,1024]{1,0:T(8,128)}, f32[1024,256]{1,0:T(8,128)})) %all-reduce.6.cloned.1.call-update) | async-done | bytes 2097168 | tf_op jit(solution)/shard_map/psum | solution.py:219
  247.4 2.4 broadcast_multiply_fusion
  249.8 1.1 broadcast_multiply_fusion.1
  (151 shorter events, 2.1 us)
Async XLA Ops:
  7.2 31.3 %copy-start = (bf16[256,1024]{1,0:T(8,128)(2,1)S(1)}, bf16[256,1024]{1,0:T(8,128)(2,1)}, u32[]{:S(2)}) copy-start(bf16[256,1024]{1,0:T(8,128)(2,1)} %param.19) | copy-start | bytes 1572868
  7.2 240.2 %all-reduce.6.cloned.1.call-start = ((), (), s32[]{:S(2)}) async-start(), calls=%async_computation | async-start | bytes 4194304 | tf_op jit(solution)/shard_map/psum | solution.py:219
  9.7 12.9 %collective-permute-start.1 = (bf16[1,16,3,256]{3,2,1,0:T(4,128)(2,1)S(1)}, bf16[1,16,3,256]{3,2,1,0:T(4,128)(2,1)S(1)}, u32[]{:S(2)}, u32[]{:S(2)}) collective-permute-start(bf16[1,16,3,256]{3,2,1,0:T(4,128)(2,1)S(1)} %get-tuple-element.105), channel_id=1, source_target_pairs={{0,2},{2,4},{4,6},{6,8},{8,10},{10,12},{12,14},{14,16},{16,18},{18... | collective-permute-start | bytes 73736 | tf_op jit(solution)/shard_map/ppermute | solution.py:16
  12.1 10.5 %collective-permute-start.2 = (bf16[1,16,3,256]{3,2,1,0:T(4,128)(2,1)S(1)}, bf16[1,16,3,256]{3,2,1,0:T(4,128)(2,1)S(1)}, u32[]{:S(2)}, u32[]{:S(2)}) collective-permute-start(bf16[1,16,3,256]{3,2,1,0:T(4,128)(2,1)S(1)} %get-tuple-element.104), channel_id=1, source_target_pairs={{2,0},{4,2},{6,4},{8,6},{10,8},{12,10},{14,12},{16,14},{18,16},{20... | collective-permute-start | bytes 73736 | tf_op jit(solution)/shard_map/ppermute | solution.py:16
  13.5 9.6 %collective-permute-start = (bf16[2,1,16,3,256]{4,3,2,1,0:T(4,128)(2,1)S(1)}, bf16[2,1,16,3,256]{4,3,2,1,0:T(4,128)(2,1)S(1)}, u32[]{:S(2)}, u32[]{:S(2)}) collective-permute-start(bf16[2,1,16,3,256]{4,3,2,1,0:T(4,128)(2,1)S(1)} %pad_maximum_fusion.1), channel_id=1, source_target_pairs={{0,16},{16,0},{2,18},{18,2},{4,20},{20,4},{6,22},{22,6},{8,24},{24... | collective-permute-start | bytes 147464 | tf_op jit(solution)/shard_map/ppermute | solution.py:26
  22.4 15.1 %copy-start.5 = (f32[1,1,256]{2,1,0:T(1,128)}, f32[1,1,256]{2,1,0:T(1,128)S(1)}, u32[]{:S(2)}) copy-start(f32[1,1,256]{2,1,0:T(1,128)S(1)} %get-tuple-element.137) | copy-start | bytes 3076
  22.4 15.1 %copy-start.7 = (f32[1,1,256]{2,1,0:T(1,128)}, f32[1,1,256]{2,1,0:T(1,128)S(1)}, u32[]{:S(2)}) copy-start(f32[1,1,256]{2,1,0:T(1,128)S(1)} %get-tuple-element.138) | copy-start | bytes 3076
  22.4 15.1 %copy-start.9 = (f32[1,1,256]{2,1,0:T(1,128)}, f32[1,1,256]{2,1,0:T(1,128)S(1)}, u32[]{:S(2)}) copy-start(f32[1,1,256]{2,1,0:T(1,128)S(1)} %get-tuple-element.139) | copy-start | bytes 3076
  22.4 15.1 %copy-start.11 = (f32[1,1,256]{2,1,0:T(1,128)}, f32[1,1,256]{2,1,0:T(1,128)S(1)}, u32[]{:S(2)}) copy-start(f32[1,1,256]{2,1,0:T(1,128)S(1)} %get-tuple-element.140) | copy-start | bytes 3076
  22.5 15.1 %copy-start.13 = (f32[1,1,256]{2,1,0:T(1,128)}, f32[1,1,256]{2,1,0:T(1,128)S(1)}, u32[]{:S(2)}) copy-start(f32[1,1,256]{2,1,0:T(1,128)S(1)} %get-tuple-element.141) | copy-start | bytes 3076
  22.5 15.1 %copy-start.15 = (f32[1,1,256]{2,1,0:T(1,128)}, f32[1,1,256]{2,1,0:T(1,128)S(1)}, u32[]{:S(2)}) copy-start(f32[1,1,256]{2,1,0:T(1,128)S(1)} %get-tuple-element.142) | copy-start | bytes 3076
  22.5 15.1 %copy-start.17 = (f32[1,1,256]{2,1,0:T(1,128)}, f32[1,1,256]{2,1,0:T(1,128)S(1)}, u32[]{:S(2)}) copy-start(f32[1,1,256]{2,1,0:T(1,128)S(1)} %get-tuple-element.143) | copy-start | bytes 3076
  22.5 15.1 %copy-start.19 = (f32[1,1,256]{2,1,0:T(1,128)}, f32[1,1,256]{2,1,0:T(1,128)S(1)}, u32[]{:S(2)}) copy-start(f32[1,1,256]{2,1,0:T(1,128)S(1)} %get-tuple-element.144) | copy-start | bytes 3076
  22.5 15.1 %copy-start.21 = (f32[1,1,256]{2,1,0:T(1,128)}, f32[1,1,256]{2,1,0:T(1,128)S(1)}, u32[]{:S(2)}) copy-start(f32[1,1,256]{2,1,0:T(1,128)S(1)} %get-tuple-element.145) | copy-start | bytes 3076
  23.6 5.4 %collective-permute-start.3 = (bf16[1,3,54,256]{3,2,1,0:T(8,128)(2,1)S(1)}, bf16[1,3,54,256]{3,2,1,0:T(8,128)(2,1)S(1)}, u32[]{:S(2)}, u32[]{:S(2)}) collective-permute-start(bf16[1,3,54,256]{3,2,1,0:T(8,128)(2,1)S(1)} %slice.869), channel_id=1, source_target_pairs={{0,16},{16,0},{2,18},{18,2},{4,20},{20,4},{6,22},{22,6},{8,24},{24... | collective-permute-start | bytes 248840 | tf_op jit(solution)/shard_map/ppermute | solution.py:26
  27.2 10.4 %copy-start.23 = (f32[1,1,256]{2,1,0:T(1,128)}, f32[1,1,256]{2,1,0:T(1,128)S(1)}, u32[]{:S(2)}) copy-start(f32[1,1,256]{2,1,0:T(1,128)S(1)} %get-tuple-element.146) | copy-start | bytes 3076
  27.2 10.4 %copy-start.25 = (f32[1,1,256]{2,1,0:T(1,128)}, f32[1,1,256]{2,1,0:T(1,128)S(1)}, u32[]{:S(2)}) copy-start(f32[1,1,256]{2,1,0:T(1,128)S(1)} %get-tuple-element.147) | copy-start | bytes 3076
  27.2 10.4 %copy-start.27 = (f32[1,1,256]{2,1,0:T(1,128)}, f32[1,1,256]{2,1,0:T(1,128)S(1)}, u32[]{:S(2)}) copy-start(f32[1,1,256]{2,1,0:T(1,128)S(1)} %get-tuple-element.148) | copy-start | bytes 3076
  27.2 10.4 %copy-start.29 = (f32[1,1,256]{2,1,0:T(1,128)}, f32[1,1,256]{2,1,0:T(1,128)S(1)}, u32[]{:S(2)}) copy-start(f32[1,1,256]{2,1,0:T(1,128)S(1)} %get-tuple-element.149) | copy-start | bytes 3076
  27.2 10.4 %copy-start.31 = (f32[1,1,256]{2,1,0:T(1,128)}, f32[1,1,256]{2,1,0:T(1,128)S(1)}, u32[]{:S(2)}) copy-start(f32[1,1,256]{2,1,0:T(1,128)S(1)} %get-tuple-element.150) | copy-start | bytes 3076
  27.2 10.4 %copy-start.33 = (f32[1,1,256]{2,1,0:T(1,128)}, f32[1,1,256]{2,1,0:T(1,128)S(1)}, u32[]{:S(2)}) copy-start(f32[1,1,256]{2,1,0:T(1,128)S(1)} %get-tuple-element.151) | copy-start | bytes 3076
  27.3 10.4 %copy-start.35 = (f32[1,1,256]{2,1,0:T(1,128)}, f32[1,1,256]{2,1,0:T(1,128)S(1)}, u32[]{:S(2)}) copy-start(f32[1,1,256]{2,1,0:T(1,128)S(1)} %get-tuple-element.152) | copy-start | bytes 3076
  27.3 10.4 %copy-start.37 = (f32[1,1,256]{2,1,0:T(1,128)}, f32[1,1,256]{2,1,0:T(1,128)S(1)}, u32[]{:S(2)}) copy-start(f32[1,1,256]{2,1,0:T(1,128)S(1)} %get-tuple-element.153) | copy-start | bytes 3076
  55.9 41.7 %copy-start.6 = (f32[1,1,256]{2,1,0:T(1,128)S(1)}, f32[1,1,256]{2,1,0:T(1,128)}, u32[]{:S(2)}) copy-start(f32[1,1,256]{2,1,0:T(1,128)} %copy-done.5) | copy-start | bytes 3076
  55.9 41.7 %copy-start.8 = (f32[1,1,256]{2,1,0:T(1,128)S(1)}, f32[1,1,256]{2,1,0:T(1,128)}, u32[]{:S(2)}) copy-start(f32[1,1,256]{2,1,0:T(1,128)} %copy-done.7) | copy-start | bytes 3076
  56.0 41.7 %copy-start.10 = (f32[1,1,256]{2,1,0:T(1,128)S(1)}, f32[1,1,256]{2,1,0:T(1,128)}, u32[]{:S(2)}) copy-start(f32[1,1,256]{2,1,0:T(1,128)} %copy-done.9) | copy-start | bytes 3076
  56.0 41.7 %copy-start.12 = (f32[1,1,256]{2,1,0:T(1,128)S(1)}, f32[1,1,256]{2,1,0:T(1,128)}, u32[]{:S(2)}) copy-start(f32[1,1,256]{2,1,0:T(1,128)} %copy-done.11) | copy-start | bytes 3076
  56.0 41.7 %copy-start.14 = (f32[1,1,256]{2,1,0:T(1,128)S(1)}, f32[1,1,256]{2,1,0:T(1,128)}, u32[]{:S(2)}) copy-start(f32[1,1,256]{2,1,0:T(1,128)} %copy-done.13) | copy-start | bytes 3076
  56.0 41.7 %copy-start.16 = (f32[1,1,256]{2,1,0:T(1,128)S(1)}, f32[1,1,256]{2,1,0:T(1,128)}, u32[]{:S(2)}) copy-start(f32[1,1,256]{2,1,0:T(1,128)} %copy-done.15) | copy-start | bytes 3076
  56.0 41.7 %copy-start.18 = (f32[1,1,256]{2,1,0:T(1,128)S(1)}, f32[1,1,256]{2,1,0:T(1,128)}, u32[]{:S(2)}) copy-start(f32[1,1,256]{2,1,0:T(1,128)} %copy-done.17) | copy-start | bytes 3076
  56.0 41.7 %copy-start.20 = (f32[1,1,256]{2,1,0:T(1,128)S(1)}, f32[1,1,256]{2,1,0:T(1,128)}, u32[]{:S(2)}) copy-start(f32[1,1,256]{2,1,0:T(1,128)} %copy-done.19) | copy-start | bytes 3076
  56.0 41.7 %copy-start.22 = (f32[1,1,256]{2,1,0:T(1,128)S(1)}, f32[1,1,256]{2,1,0:T(1,128)}, u32[]{:S(2)}) copy-start(f32[1,1,256]{2,1,0:T(1,128)} %copy-done.21) | copy-start | bytes 3076
  56.0 41.7 %copy-start.24 = (f32[1,1,256]{2,1,0:T(1,128)S(1)}, f32[1,1,256]{2,1,0:T(1,128)}, u32[]{:S(2)}) copy-start(f32[1,1,256]{2,1,0:T(1,128)} %copy-done.23) | copy-start | bytes 3076
  56.0 41.7 %copy-start.26 = (f32[1,1,256]{2,1,0:T(1,128)S(1)}, f32[1,1,256]{2,1,0:T(1,128)}, u32[]{:S(2)}) copy-start(f32[1,1,256]{2,1,0:T(1,128)} %copy-done.25) | copy-start | bytes 3076
  56.0 41.7 %copy-start.28 = (f32[1,1,256]{2,1,0:T(1,128)S(1)}, f32[1,1,256]{2,1,0:T(1,128)}, u32[]{:S(2)}) copy-start(f32[1,1,256]{2,1,0:T(1,128)} %copy-done.27) | copy-start | bytes 3076
  56.1 41.7 %copy-start.30 = (f32[1,1,256]{2,1,0:T(1,128)S(1)}, f32[1,1,256]{2,1,0:T(1,128)}, u32[]{:S(2)}) copy-start(f32[1,1,256]{2,1,0:T(1,128)} %copy-done.29) | copy-start | bytes 3076
  56.1 41.7 %copy-start.32 = (f32[1,1,256]{2,1,0:T(1,128)S(1)}, f32[1,1,256]{2,1,0:T(1,128)}, u32[]{:S(2)}) copy-start(f32[1,1,256]{2,1,0:T(1,128)} %copy-done.31) | copy-start | bytes 3076
  56.1 41.7 %copy-start.34 = (f32[1,1,256]{2,1,0:T(1,128)S(1)}, f32[1,1,256]{2,1,0:T(1,128)}, u32[]{:S(2)}) copy-start(f32[1,1,256]{2,1,0:T(1,128)} %copy-done.33) | copy-start | bytes 3076
  56.1 41.7 %copy-start.36 = (f32[1,1,256]{2,1,0:T(1,128)S(1)}, f32[1,1,256]{2,1,0:T(1,128)}, u32[]{:S(2)}) copy-start(f32[1,1,256]{2,1,0:T(1,128)} %copy-done.35) | copy-start | bytes 3076
  56.1 41.7 %copy-start.38 = (f32[1,1,256]{2,1,0:T(1,128)S(1)}, f32[1,1,256]{2,1,0:T(1,128)}, u32[]{:S(2)}) copy-start(f32[1,1,256]{2,1,0:T(1,128)} %copy-done.37) | copy-start | bytes 3076
  56.1 41.7 %copy-start.40 = (f32[1,1,256]{2,1,0:T(1,128)S(1)}, f32[1,1,256]{2,1,0:T(1,128)}, u32[]{:S(2)}) copy-start(f32[1,1,256]{2,1,0:T(1,128)} %copy-done.39) | copy-start | bytes 3076
  56.1 41.7 %copy-start.42 = (f32[1,1,256]{2,1,0:T(1,128)S(1)}, f32[1,1,256]{2,1,0:T(1,128)}, u32[]{:S(2)}) copy-start(f32[1,1,256]{2,1,0:T(1,128)} %copy-done.41) | copy-start | bytes 3076
  56.1 41.7 %copy-start.44 = (f32[1,1,256]{2,1,0:T(1,128)S(1)}, f32[1,1,256]{2,1,0:T(1,128)}, u32[]{:S(2)}) copy-start(f32[1,1,256]{2,1,0:T(1,128)} %copy-done.43) | copy-start | bytes 3076
  108.1 6.0 %collective-permute-start.4 = (bf16[1,3,54,256]{3,2,1,0:T(8,128)(2,1)S(1)}, bf16[1,3,54,256]{3,2,1,0:T(8,128)(2,1)S(1)}, u32[]{:S(2)}, u32[]{:S(2)}) collective-permute-start(bf16[1,3,54,256]{3,2,1,0:T(8,128)(2,1)S(1)} %fusion.230), channel_id=1, source_target_pairs={{0,16},{16,0},{2,18},{18,2},{4,20},{20,4},{6,22},{22,6},{8,24},{24... | collective-permute-start | bytes 248840 | tf_op jit(solution)/shard_map/ppermute | solution.py:26
  111.8 12.0 %copy-start.2 = (bf16[768,256]{1,0:T(8,128)(2,1)S(1)}, bf16[768,256]{1,0:T(8,128)(2,1)}, u32[]{:S(2)}) copy-start(bf16[768,256]{1,0:T(8,128)(2,1)} %get-tuple-element.102) | copy-start | bytes 1179652
  114.2 15.1 %collective-permute-start.6 = (bf16[1,16,3,256]{3,2,1,0:T(4,128)(2,1)S(1)}, bf16[1,16,3,256]{3,2,1,0:T(4,128)(2,1)S(1)}, u32[]{:S(2)}, u32[]{:S(2)}) collective-permute-start(bf16[1,16,3,256]{3,2,1,0:T(4,128)(2,1)S(1)} %get-tuple-element.100), channel_id=1, source_target_pairs={{0,2},{2,4},{4,6},{6,8},{8,10},{10,12},{12,14},{14,16},{16,18},{18... | collective-permute-start | bytes 73736 | tf_op jit(solution)/shard_map/ppermute | solution.py:16
  115.5 13.8 %collective-permute-start.7 = (bf16[1,16,3,256]{3,2,1,0:T(4,128)(2,1)S(1)}, bf16[1,16,3,256]{3,2,1,0:T(4,128)(2,1)S(1)}, u32[]{:S(2)}, u32[]{:S(2)}) collective-permute-start(bf16[1,16,3,256]{3,2,1,0:T(4,128)(2,1)S(1)} %get-tuple-element.99), channel_id=1, source_target_pairs={{2,0},{4,2},{6,4},{8,6},{10,8},{12,10},{14,12},{16,14},{18,16},{20... | collective-permute-start | bytes 73736 | tf_op jit(solution)/shard_map/ppermute | solution.py:16
  116.8 12.4 %collective-permute-start.5 = (bf16[2,1,16,3,256]{4,3,2,1,0:T(4,128)(2,1)S(1)}, bf16[2,1,16,3,256]{4,3,2,1,0:T(4,128)(2,1)S(1)}, u32[]{:S(2)}, u32[]{:S(2)}) collective-permute-start(bf16[2,1,16,3,256]{4,3,2,1,0:T(4,128)(2,1)S(1)} %pad_maximum_fusion.2), channel_id=1, source_target_pairs={{0,16},{16,0},{2,18},{18,2},{4,20},{20,4},{6,22},{22,6},{8,24},{24... | collective-permute-start | bytes 147464 | tf_op jit(solution)/shard_map/ppermute | solution.py:26
  (13 other events, 60.3 us)
Sparse Core Ops, SparseCore 0:
  111.9 135.4 all-reduce.5
where the time goes:
time: 258 us
  waiting for transfers between devices  125 us (48%)
  blocking collectives  40.4 us (16%)
  other arithmetic  33.3 us (13%)
  starting transfers between devices  25.2 us (10%)
  between operations  15.8 us (6%)
  matrix products  10.9 us (4%)
  local copies, waits for them, and re-layouts  7.37 us (3%)
    psum x1, waiting for transfers between devices, shards(): lax.psum((kernel_part, gain_part, w_in_part, w_out_part, scale_part), ('t...  116 us
    psum x1, blocking collectives, shards(): lax.psum((kernel_part, gain_part, w_in_part, w_out_part, scale_part), ('t...  40.4 us
    ppermute x4, starting transfers between devices, from_partner(): return lax.ppermute(block, axis, route)  18.9 us
    add x1, other arithmetic, spread(): running = running + kernel_f[row_shift, col_shift] * window  10 us
    ppermute x4, waiting for transfers between devices, from_partner(): return lax.ppermute(block, axis, route)  8.19 us
    reduce_sum x1, other arithmetic, block_step(): row_mean = jnp.mean(convolved, axis=-1, keepdims=True)  8.17 us
    ppermute x4, starting transfers between devices, passed_along(): return lax.ppermute(block, axis, route)  6.23 us
    reduce_sum x4, other arithmetic, kernel_terms(): taps.append(jnp.sum(grad_f * window.astype(jnp.float32), axis=leading))  5.92 us
  transfers between devices with their start and end apart: 9, of which 5 were waited for; matrix products, arithmetic and copies ran while one was open for 3% of the time, Pallas kernels for 0%

commit v1 on v0

--- a/solution.py
+++ b/solution.py
@@ -1,10 +1,11 @@
 import jax
 import jax.numpy as jnp
 from jax import lax
-from jax.sharding import PartitionSpec as P
+from jax.sharding import Mesh, PartitionSpec as P
 
 HID = 1024
 KSIZE = 7
+TILES = ("chips", "core")
 
 
 EPS = 1e-06
@@ -122,12 +123,57 @@
     return block_step
 
 
+def summed(kernel_part, gain_part, w_in_part, w_out_part, scale_part):
+    channels = kernel_part.shape[-1]
+    chips = lax.axis_size(TILES) // 2 * lax.axis_size("dp")
+    core = lax.axis_index(TILES) % 2
+    big = jnp.concatenate(
+        [w_in_part.reshape(channels, -1, channels).transpose(1, 0, 2).reshape(-1, channels), w_out_part]
+    )
+    rows = big.shape[0] // 2
+    halves = big.reshape(2, rows, channels)
+    keep = lax.dynamic_index_in_dim(halves, core, 0, keepdims=False)
+    give = lax.dynamic_index_in_dim(halves, 1 - core, 0, keepdims=False).astype(jnp.bfloat16)
+    mine = keep + core_swap(give).astype(jnp.float32)
+    small = jnp.concatenate(
+        [kernel_part.reshape(-1, channels), gain_part[None], scale_part[None]]
+    )
+    small_rows = -(-small.shape[0] // chips) * chips
+    small = jnp.pad(small, ((0, small_rows - small.shape[0]), (0, 0)))
+    pieces = jnp.concatenate(
+        [mine.reshape(chips, -1, channels), small.reshape(chips, -1, channels)], axis=1
+    ).astype(jnp.bfloat16)
+    axes = ("chips", "dp")
+    got = lax.all_to_all(pieces, axes, 0, 0, tiled=True)
+    total = jnp.sum(got.astype(jnp.float32), axis=0).astype(jnp.bfloat16)
+    every = lax.all_to_all(jnp.broadcast_to(total, got.shape), axes, 0, 0, tiled=True)
+    other = core_swap(every)
+    cut = rows // chips
+    low = jnp.where(core == 0, every, other)[:, :cut].reshape(rows, channels)
+    high = jnp.where(core == 0, other, every)[:, :cut].reshape(rows, channels)
+    every_f = every[:, cut:].astype(jnp.float32) + other[:, cut:].astype(jnp.float32)
+    small_sum = every_f.reshape(small_rows, channels)
+    taps = KSIZE * KSIZE
+    w_in_sum = low.reshape(-1, channels, channels).transpose(1, 0, 2).reshape(channels, -1)
+    return (
+        small_sum[:taps].reshape(kernel_part.shape),
+        small_sum[taps],
+        w_in_sum.astype(jnp.float32),
+        high.astype(jnp.float32),
+        small_sum[taps + 1],
+    )
+
+
+def core_swap(block):
+    return lax.ppermute(block, "core", [(0, 1), (1, 0)])
+
+
 def shards(fields, grad_out, block_count, ocean, kernel, ln_gain, w_in, w_out, layer_scale):
     samples, slot_count, tile_rows, tile_cols, channels = fields.shape
     half_kernel = KSIZE // 2
-    half_axis = lax.axis_size("tiles") // 2
-    top_bit = lax.axis_size("tiles").bit_length() - 2
-    here = lax.axis_index("tiles")
+    half_axis = lax.axis_size(TILES) // 2
+    top_bit = lax.axis_size(TILES).bit_length() - 2
+    here = lax.axis_index(TILES)
     lower_half = here < half_axis
     at_start = here % half_axis == 0
     at_end = here % half_axis == half_axis - 1
@@ -150,9 +196,9 @@
     right_edge = lax.dynamic_slice_in_dim(strip, used_cols - half_kernel, half_kernel, 2)
     up_send = jnp.where(lower_half, right_edge, left_edge)
     down_send = jnp.where(lower_half, left_edge, right_edge)
-    from_lower = passed_along(up_send, "tiles", 1)
-    from_upper = passed_along(down_send, "tiles", -1)
-    far_edges = from_partner(jnp.stack([down_send, up_send]), "tiles", top_bit)
+    from_lower = passed_along(up_send, TILES, 1)
+    from_upper = passed_along(down_send, TILES, -1)
+    far_edges = from_partner(jnp.stack([down_send, up_send]), TILES, top_bit)
     from_lower = jnp.where(at_start, far_edges[0], from_lower)
     from_upper = jnp.where(at_end, far_edges[1], from_upper)
     from_west = jnp.where(lower_half, from_lower, from_upper)
@@ -160,7 +206,7 @@
     blank_cols = jnp.zeros((samples, tile_rows, half_kernel, channels), jnp.bfloat16)
     extended = jnp.concatenate([from_west, strip, blank_cols], axis=2)
     extended = lax.dynamic_update_slice_in_dim(extended, from_east, used_cols + half_kernel, 2)
-    mirrored = from_partner(extended[:, tile_rows - half_kernel :], "tiles", top_bit)
+    mirrored = from_partner(extended[:, tile_rows - half_kernel :], TILES, top_bit)
     north_rows = jnp.roll(mirrored[:, ::-1, ::-1], used_cols - strip_width, axis=2)
     south_rows = jnp.zeros(
         (samples, half_kernel, strip_width + 2 * half_kernel, channels), jnp.bfloat16
@@ -191,7 +237,7 @@
     north_grad = dpadded[:, tile_rows + half_kernel :]
     returned = from_partner(
         jnp.roll(north_grad[:, ::-1, ::-1], used_cols - strip_width, axis=2).astype(jnp.bfloat16),
-        "tiles",
+        TILES,
         top_bit,
     ).astype(jnp.float32)
     dextended = dpadded[:, half_kernel : tile_rows + half_kernel]
@@ -201,10 +247,10 @@
     core_grad = dextended[:, :, half_kernel : strip_width + half_kernel]
     up_grad = jnp.where(lower_half, east_grad, west_grad)
     down_grad = jnp.where(lower_half, west_grad, east_grad)
-    grad_lower = passed_along(up_grad.astype(jnp.bfloat16), "tiles", 1).astype(up_grad.dtype)
-    grad_upper = passed_along(down_grad.astype(jnp.bfloat16), "tiles", -1).astype(down_grad.dtype)
+    grad_lower = passed_along(up_grad.astype(jnp.bfloat16), TILES, 1).astype(up_grad.dtype)
+    grad_upper = passed_along(down_grad.astype(jnp.bfloat16), TILES, -1).astype(down_grad.dtype)
     far_grads = from_partner(
-        jnp.stack([down_grad, up_grad]).astype(jnp.bfloat16), "tiles", top_bit
+        jnp.stack([down_grad, up_grad]).astype(jnp.bfloat16), TILES, top_bit
     ).astype(jnp.float32)
     grad_lower = jnp.where(at_start, far_grads[0], grad_lower)
     grad_upper = jnp.where(at_end, far_grads[1], grad_upper)
@@ -216,11 +262,11 @@
     )
     core_grad = lax.dynamic_update_slice_in_dim(core_grad, tail_cols, used_cols - half_kernel, 2)
     grad_strip = (mask_strip * (tangent.astype(jnp.float32) + core_grad)).astype(jnp.bfloat16)
-    kernel_sum, gain_sum, w_in_sum, w_out_sum, scale_sum = lax.psum(
-        (kernel_part, gain_part, w_in_part, w_out_part, scale_part), ("tiles", "dp")
+    kernel_sum, gain_sum, w_in_sum, w_out_sum, scale_sum = summed(
+        kernel_part, gain_part, w_in_part, w_out_part, scale_part
     )
     norm = (
-        samples * lax.axis_size("dp") * slot_count * lax.axis_size("tiles") * tile_rows * tile_cols
+        samples * lax.axis_size("dp") * slot_count * lax.axis_size(TILES) * tile_rows * tile_cols
     ) ** (-0.5)
     state_next = jnp.transpose(
         outputs[0].reshape(samples, tile_rows, slot_count, tile_cols, channels), (0, 2, 1, 3, 4)
@@ -240,11 +286,12 @@
 
 
 def solution(mesh):
+    cores = Mesh(mesh.devices.reshape(-1, 2, mesh.devices.shape[1]), ("chips", "core", "dp"))
     placed = (
-        P("dp", "tiles", None, None, None),
-        P("dp", "tiles", None, None, None),
-        P("tiles"),
-        P("tiles"),
+        P("dp", TILES, None, None, None),
+        P("dp", TILES, None, None, None),
+        P(TILES),
+        P(TILES),
         P(),
         P(),
         P(),
@@ -253,11 +300,11 @@
     )
     return jax.shard_map(
         shards,
-        mesh=mesh,
+        mesh=cores,
         in_specs=placed,
         out_specs=(
-            P("dp", "tiles", None, None, None),
-            P("dp", "tiles", None, None, None),
+            P("dp", TILES, None, None, None),
+            P("dp", TILES, None, None, None),
             P(),
             P(),
             P(),

time: 258 us -> 164 us (0.64)
  waiting for transfers between devices: 125 us -> 21.3 us
  local copies, waits for them, and re-layouts: 7.37 us -> 54.2 us
  blocking collectives: 40.4 us -> 0 us
  between operations: 15.8 us -> 3.1 us
  starting transfers between devices: 25.2 us -> 33.3 us
  other arithmetic: 33.3 us -> 39.4 us
    psum x1 -> x0, waiting for transfers between devices: 116 us -> none  [shards(): lax.psum((kernel_part, gain_part, w_in_part, w_out_part, scale_part), ('t...]
    psum x1 -> x0, blocking collectives: 40.4 us -> none  [shards(): lax.psum((kernel_part, gain_part, w_in_part, w_out_part, scale_part), ('t...]
    another operation x7 -> x56, local copies, waits for them, and re-layouts: 0.2 us -> 27.7 us  [kernel_terms(): stacked.append(jnp.stack(taps))]
    all_to_all x0 -> x2, waiting for transfers between devices: none -> 16.1 us  [the longest x1 16.1 us: summed(): got = lax.all_to_all(pieces, axes, 0, 0, tiled=True)]
    all_to_all x0 -> x2, starting transfers between devices: none -> 9.94 us  [the longest x1 5.42 us: summed(): got = lax.all_to_all(pieces, axes, 0, 0, tiled=True)]
    ppermute x4, starting transfers between devices: 18.9 us -> 11.6 us  [from_partner(): return lax.ppermute(block, axis, route)]
    unnamed x111 -> x180, local copies, waits for them, and re-layouts: 1.17 us -> 7.62 us
    ppermute x4, starting transfers between devices: 6.23 us -> 9.24 us  [passed_along(): return lax.ppermute(block, axis, route)]
  transfers between devices with their start and end apart: 9 -> 12, of which waited for: 5 -> 4; matrix products, arithmetic and copies ran while one was open for 3% -> 24% of each run, Pallas kernels for 0% -> 0%
where the time goes in v1:
time: 164 us; the launch traced here: 163 us
  local copies, waits for them, and re-layouts  54.2 us (33%)
  other arithmetic  39.4 us (24%)
  starting transfers between devices  33.3 us (20%)
  waiting for transfers between devices  21.3 us (13%)
  matrix products  11.3 us (7%)
  between operations  3.1 us (2%)
    another operation x56, local copies, waits for them, and re-layouts, kernel_terms(): stacked.append(jnp.stack(taps))  27.7 us
    all_to_all x1, waiting for transfers between devices, summed(): got = lax.all_to_all(pieces, axes, 0, 0, tiled=True)  16.1 us
    ppermute x4, starting transfers between devices, from_partner(): return lax.ppermute(block, axis, route)  11.6 us
    add x1, other arithmetic, spread(): running = running + kernel_f[row_shift, col_shift] * window  10.9 us
    ppermute x4, starting transfers between devices, passed_along(): return lax.ppermute(block, axis, route)  9.24 us
    reduce_sum x1, other arithmetic, block_step(): row_mean = jnp.mean(convolved, axis=-1, keepdims=True)  8.79 us
    unnamed x180, local copies, waits for them, and re-layouts  7.62 us
    reduce_sum x4, other arithmetic, kernel_terms(): taps.append(jnp.sum(grad_f * window.astype(jnp.float32), axis=leading))  5.93 us
  transfers between devices with their start and end apart: 12, of which 4 were waited for; matrix products, arithmetic and copies ran while one was open for 24% of the time, Pallas kernels for 0%

profile of v1, /device:TPU:0, one launch (start us, length us, event | category | flops | bytes accessed | tf_op | source)
XLA Modules:
  0.0 162.6 jit_solution(12241534620819495462)
XLA Ops:
  1.4 1.1 fusion.264
  2.5 1.1 copy_multiply_fusion
  3.7 1.3 collective-permute-start.2
  5.0 3.0 %collective-permute-start.1 = (bf16[1,16,3,256]{3,2,1,0:T(4,128)(2,1)S(1)}, bf16[1,16,3,256]{3,2,1,0:T(4,128)(2,1)S(1)}, u32[]{:S(2)}, u32[]{:S(2)}) collective-permute-start(bf16[1,16,3,256]{3,2,1,0:T(4,128)(2,1)S(1)} %get-tuple-element.123), channel_id=1, source_target_pairs={{0,2},{2,4},{4,6},{6,8},{8,10},{10,12},{12,14},{14,16},{16,18},{18... | collective-permute-start | bytes 73736 | tf_op jit(solution)/shard_map/ppermute | solution.py:17
  8.0 4.4 %collective-permute-start = (bf16[2,1,16,3,256]{4,3,2,1,0:T(4,128)(2,1)S(1)}, bf16[2,1,16,3,256]{4,3,2,1,0:T(4,128)(2,1)S(1)}, u32[]{:S(2)}, u32[]{:S(2)}) collective-permute-start(bf16[2,1,16,3,256]{4,3,2,1,0:T(4,128)(2,1)S(1)} %pad_maximum_fusion.3), channel_id=1, source_target_pairs={{0,16},{16,0},{2,18},{18,2},{4,20},{20,4},{6,22},{22,6},{8,24},{24... | collective-permute-start | bytes 147464 | tf_op jit(solution)/shard_map/ppermute | solution.py:27
  12.5 1.0 fusion.266
  13.7 1.0 fusion.265
  15.8 3.0 %collective-permute-start.3 = (bf16[1,3,54,256]{3,2,1,0:T(8,128)(2,1)S(1)}, bf16[1,3,54,256]{3,2,1,0:T(8,128)(2,1)S(1)}, u32[]{:S(2)}, u32[]{:S(2)}) collective-permute-start(bf16[1,3,54,256]{3,2,1,0:T(8,128)(2,1)S(1)} %slice.897), channel_id=1, source_target_pairs={{0,16},{16,0},{2,18},{18,2},{4,20},{20,4},{6,22},{22,6},{8,24},{24... | collective-permute-start | bytes 248840 | tf_op jit(solution)/shard_map/ppermute | solution.py:27
  18.9 1.6 fusion.267
  22.2 8.8 %fusion.262 = (f32[16,48]{1,0:T(8,128)S(1)}, f32[1,16,48,256]{3,2,1,0:T(8,128)S(1)}) fusion(bf16[1,3,54,256]{3,2,1,0:T(8,128)(2,1)S(1)} %fusion.246, bf16[1,16,54,256]{3,2,1,0:T(8,128)(2,1)S(1)} %dynamic_update_slice.6, f32[256]{0:T(256)} %bitcast.57, f32[256]{0:T(256)} %bitcast.56, f32[256]{0:T(256)} %bitcast.55, f32[256]{0:T(256)} %bitcast.54, ...), kind=kLoop, calls=%fused_computation.493 | loop fusion | flops 41286912 | bytes 4136960 | tf_op jit(solution)/shard_map/reduce_sum | solution.py:84
  32.9 1.2 multiply_convert_fusion
  34.1 1.4 fusion.220
  35.5 1.6 fusion.269
  37.1 3.4 %fusion.13 = (bf16[1024,768]{0,1:T(8,128)(2,1)}, f32[768,1024]{1,0:T(8,128)S(1)}) fusion(f32[768,1024]{1,0:T(8,128)S(1)} %get-tuple-element.178, bf16[768,256]{1,0:T(8,128)(2,1)S(1)} %get-tuple-element.121, bf16[1024,256]{1,0:T(8,128)(2,1)S(1)} %copy-done), kind=kOutput, calls=%fused_computation.135 | convolution fusion | flops 418381824 | bytes 8781824 | tf_op jit(solution)/shard_map/dot_general | solution.py:102
  40.5 3.0 %multiply_reduce_fusion = (bf16[256]{0:T(256)(128)(2,1)}, f32[768]{0:T(1024)S(1)}, f32[768]{0:T(1024)S(1)}, f32[768,256]{1,0:T(8,128)S(1)}) fusion(f32[1,16,48,256]{3,2,1,0:T(8,128)S(1)} %get-tuple-element.112, f32[768]{0:T(1024)S(1)} %rsqrt.13, f32[768]{0:T(1024)S(1)} %div.15, f32[256]{0:T(256)S(1)} %copy-done.4, bf16[256,1024]{1,0:T(8,128)(2,1)S(1)} %copy-done.83, ...), kind=kOutput, calls=%fused_computation.405 | convolution fusion | flops 419952896 | bytes 8402432 | tf_op jit(solution)/shard_map/dot_general | solution.py:110
  44.1 1.2 fusion.212
  45.3 1.2 fusion.213
  46.5 1.8 %fusion.211 = (bf16[256]{0:T(256)(128)(2,1)S(1)}, bf16[256]{0:T(256)(128)(2,1)S(1)}, bf16[256]{0:T(256)(128)(2,1)S(1)}, bf16[256]{0:T(256)(128)(2,1)S(1)}, bf16[...) fusion(bf16[1,16,48,256]{3,2,1,0:T(8,128)(2,1)S(1)} %bitcast.20, ...), kind=kLoop, calls=%fused_computation.389 | loop fusion | flops 10809600 | bytes 926208 | tf_op jit(solution)/shard_map/reduce_sum | solution.py:55
  48.3 1.7 %fusion.192 = (bf16[256]{0:T(256)(128)(2,1)S(1)}, bf16[256]{0:T(256)(128)(2,1)S(1)}, bf16[256]{0:T(256)(128)(2,1)S(1)}, bf16[256]{0:T(256)(128)(2,1)S(1)}, bf16[...) fusion(bf16[1,16,48,256]{3,2,1,0:T(8,128)(2,1)S(1)} %bitcast.20, ...), kind=kLoop, calls=%fused_computation.370 | loop fusion | flops 9629696 | bytes 3612672 | tf_op jit(solution)/shard_map/reduce_sum | solution.py:55
  50.6 1.7 %copy.59 = bf16[1024,768]{1,0:T(8,128)(2,1)S(1)} copy(bf16[1024,768]{0,1:T(8,128)(2,1)} %get-tuple-element.180) | data formatting | bytes 3145728 | tf_op jit(solution)/shard_map/dot_general | solution.py:107
  78.3 0.9 fusion.222
  79.2 2.0 %collective-permute-start.8 = (bf16[1024,256]{1,0:T(8,128)(2,1)}, bf16[1024,256]{1,0:T(8,128)(2,1)S(1)}, u32[]{:S(2)}, u32[]{:S(2)}) collective-permute-start(bf16[1024,256]{1,0:T(8,128)(2,1)} %fusion.222), channel_id=1, source_target_pairs={{0,2},{2,0},{1,3},{3,1},{4,6},{6,4},{5,7},{7,5},{8,10},{10,8},{9,1... | collective-permute-start | bytes 1572872 | tf_op jit(solution)/shard_map/ppermute | solution.py:168
  81.2 0.7 stack.296
  83.8 0.7 stack.314
  89.1 1.4 reshape.537
  90.4 1.4 fusion.253
  91.8 1.4 reshape.538
  94.0 0.9 pad_maximum_fusion.1
  94.8 5.4 %all-to-all-start = ((bf16[16,68,256]{2,1,0:T(8,128)(2,1)}), bf16[16,68,256]{2,1,0:T(8,128)(2,1)S(1)}, u32[]{:S(2)}, u32[]{:S(2)}) async-start(bf16[16,68,256]{2,1,0:T(8,128)(2,1)} %pad_maximum_fusion.1), calls=%async_computation | async-start | bytes 1179648 | tf_op jit(solution)/shard_map/all_to_all | solution.py:147
  100.7 16.1 %all-to-all-done = bf16[16,68,256]{2,1,0:T(8,128)(2,1)S(1)} async-done(((bf16[16,68,256]{2,1,0:T(8,128)(2,1)}), bf16[16,68,256]{2,1,0:T(8,128)(2,1)S(1)}, u32[]{:S(2)}, u32[]{:S(2)}) %all-to-all-start) | async-done | bytes 557088 | tf_op jit(solution)/shard_map/all_to_all | solution.py:147
  116.9 0.9 broadcast_in_dim.43
  117.8 4.5 %all-to-all-start.1 = ((bf16[16,68,256]{2,1,0:T(8,128)(2,1)}), bf16[16,68,256]{2,1,0:T(8,128)(2,1)S(1)}, u32[]{:S(2)}, u32[]{:S(2)}) async-start(bf16[16,68,256]{2,1,0:T(8,128)(2,1)} %broadcast_in_dim.43), calls=%async_computation.1 | async-start | bytes 1179648 | tf_op jit(solution)/shard_map/all_to_all | solution.py:149
  122.7 10.9 %fusion.112 = f32[1,22,54,256]{3,2,1,0:T(8,128)S(1)} fusion(f32[1,16,48,256]{3,2,1,0:T(8,128)S(1)} %convert.297, f32[256]{0:T(256)} %bitcast.57, f32[256]{0:T(256)} %bitcast.56, f32[256]{0:T(256)} %bitcast.55, f32[256]{0:T(256)} %bitcast.54, f32[256]{0:T(256)} %bitcast.53, f32[256]{0:T(256)} %bitcast.52, f32[256]{0:T(256)} %bitcast.51, f32[256]{0:T(256)} %bitcast.50, ...), kind=kLoop, calls=%fused_computation.237 | loop fusion | flops 29500416 | bytes 2053120 | tf_op jit(solution)/shard_map/add | solution.py:76
  133.9 2.9 %collective-permute-start.4 = (bf16[1,3,54,256]{3,2,1,0:T(8,128)(2,1)S(1)}, bf16[1,3,54,256]{3,2,1,0:T(8,128)(2,1)S(1)}, u32[]{:S(2)}, u32[]{:S(2)}) collective-permute-start(bf16[1,3,54,256]{3,2,1,0:T(8,128)(2,1)S(1)} %fusion.244), channel_id=1, source_target_pairs={{0,16},{16,0},{2,18},{18,2},{4,20},{20,4},{6,22},{22,6},{8,24},{24... | collective-permute-start | bytes 248840 | tf_op jit(solution)/shard_map/ppermute | solution.py:27
  136.9 4.2 %collective-permute-done.4 = bf16[1,3,54,256]{3,2,1,0:T(8,128)(2,1)S(1)} collective-permute-done((bf16[1,3,54,256]{3,2,1,0:T(8,128)(2,1)S(1)}, bf16[1,3,54,256]{3,2,1,0:T(8,128)(2,1)S(1)}, u32[]{:S(2)}, u32[]{:S(2)}) %collective-permute-start.4) | collective-permute-done | bytes 82976 | tf_op jit(solution)/shard_map/ppermute | solution.py:27
  141.8 0.8 pad_maximum_fusion.4
  142.6 1.3 collective-permute-start.5
  143.9 1.3 collective-permute-start.7
  145.2 3.6 %collective-permute-start.6 = (bf16[1,16,3,256]{3,2,1,0:T(4,128)(2,1)}, bf16[1,16,3,256]{3,2,1,0:T(4,128)(2,1)}, u32[]{:S(2)}, u32[]{:S(2)}) collective-permute-start(bf16[1,16,3,256]{3,2,1,0:T(4,128)(2,1)} %get-tuple-element.118), channel_id=1, source_target_pairs={{0,2},{2,4},{4,6},{6,8},{8,10},{10,12},{12,14},{14,16},{16,18},{18... | collective-permute-start | bytes 73736 | tf_op jit(solution)/shard_map/ppermute | solution.py:17
  149.5 1.8 %copy.71 = bf16[1,16,3,16,256]{4,3,1,2,0:T(8,128)(2,1)} copy(bf16[1,16,3,16,256]{4,3,2,1,0:T(8,128)(2,1)} %bitcast.219) | data formatting | bytes 786432 | tf_op jit(solution)/shard_map/reshape | solution.py:272
  151.4 0.9 copy.50
  152.8 1.4 slice_add_fusion.1
  154.3 1.0 scatter-add.9
  155.3 0.8 select_add_fusion
  156.4 1.2 fusion.215
  157.6 0.8 copy.55
  159.7 1.3 convert_multiply_fusion.49
  161.3 1.3 copy.56
  (291 shorter events, 43.0 us)
Async XLA Ops:
  0.6 33.4 %copy-start = (bf16[1024,256]{1,0:T(8,128)(2,1)S(1)}, bf16[1024,256]{1,0:T(8,128)(2,1)}, u32[]{:S(2)}) copy-start(bf16[1024,256]{1,0:T(8,128)(2,1)} %param.20) | copy-start | bytes 1572868
  3.7 11.3 %collective-permute-start.2 = (bf16[1,16,3,256]{3,2,1,0:T(4,128)(2,1)S(1)}, bf16[1,16,3,256]{3,2,1,0:T(4,128)(2,1)S(1)}, u32[]{:S(2)}, u32[]{:S(2)}) collective-permute-start(bf16[1,16,3,256]{3,2,1,0:T(4,128)(2,1)S(1)} %get-tuple-element.122), channel_id=1, source_target_pairs={{2,0},{4,2},{6,4},{8,6},{10,8},{12,10},{14,12},{16,14},{18,16},{20... | collective-permute-start | bytes 73736 | tf_op jit(solution)/shard_map/ppermute | solution.py:17
  5.0 10.0 %collective-permute-start.1 = (bf16[1,16,3,256]{3,2,1,0:T(4,128)(2,1)S(1)}, bf16[1,16,3,256]{3,2,1,0:T(4,128)(2,1)S(1)}, u32[]{:S(2)}, u32[]{:S(2)}) collective-permute-start(bf16[1,16,3,256]{3,2,1,0:T(4,128)(2,1)S(1)} %get-tuple-element.123), channel_id=1, source_target_pairs={{0,2},{2,4},{4,6},{6,8},{8,10},{10,12},{12,14},{14,16},{16,18},{18... | collective-permute-start | bytes 73736 | tf_op jit(solution)/shard_map/ppermute | solution.py:17
  8.0 7.2 %collective-permute-start = (bf16[2,1,16,3,256]{4,3,2,1,0:T(4,128)(2,1)S(1)}, bf16[2,1,16,3,256]{4,3,2,1,0:T(4,128)(2,1)S(1)}, u32[]{:S(2)}, u32[]{:S(2)}) collective-permute-start(bf16[2,1,16,3,256]{4,3,2,1,0:T(4,128)(2,1)S(1)} %pad_maximum_fusion.3), channel_id=1, source_target_pairs={{0,16},{16,0},{2,18},{18,2},{4,20},{20,4},{6,22},{22,6},{8,24},{24... | collective-permute-start | bytes 147464 | tf_op jit(solution)/shard_map/ppermute | solution.py:27
  15.8 6.1 %collective-permute-start.3 = (bf16[1,3,54,256]{3,2,1,0:T(8,128)(2,1)S(1)}, bf16[1,3,54,256]{3,2,1,0:T(8,128)(2,1)S(1)}, u32[]{:S(2)}, u32[]{:S(2)}) collective-permute-start(bf16[1,3,54,256]{3,2,1,0:T(8,128)(2,1)S(1)} %slice.897), channel_id=1, source_target_pairs={{0,16},{16,0},{2,18},{18,2},{4,20},{20,4},{6,22},{22,6},{8,24},{24... | collective-permute-start | bytes 248840 | tf_op jit(solution)/shard_map/ppermute | solution.py:27
  79.2 14.0 %collective-permute-start.8 = (bf16[1024,256]{1,0:T(8,128)(2,1)}, bf16[1024,256]{1,0:T(8,128)(2,1)S(1)}, u32[]{:S(2)}, u32[]{:S(2)}) collective-permute-start(bf16[1024,256]{1,0:T(8,128)(2,1)} %fusion.222), channel_id=1, source_target_pairs={{0,2},{2,0},{1,3},{3,1},{4,6},{6,4},{5,7},{7,5},{8,10},{10,8},{9,1... | collective-permute-start | bytes 1572872 | tf_op jit(solution)/shard_map/ppermute | solution.py:168
  94.8 22.0 %all-to-all-start = ((bf16[16,68,256]{2,1,0:T(8,128)(2,1)}), bf16[16,68,256]{2,1,0:T(8,128)(2,1)S(1)}, u32[]{:S(2)}, u32[]{:S(2)}) async-start(bf16[16,68,256]{2,1,0:T(8,128)(2,1)} %pad_maximum_fusion.1), calls=%async_computation | async-start | bytes 1179648 | tf_op jit(solution)/shard_map/all_to_all | solution.py:147
  100.3 22.0 %copy-start.6 = (f32[1,1,256]{2,1,0:T(1,128)S(1)}, f32[1,1,256]{2,1,0:T(1,128)}, u32[]{:S(2)}) copy-start(f32[1,1,256]{2,1,0:T(1,128)} %copy-done.5) | copy-start | bytes 3076
  100.3 22.0 %copy-start.8 = (f32[1,1,256]{2,1,0:T(1,128)S(1)}, f32[1,1,256]{2,1,0:T(1,128)}, u32[]{:S(2)}) copy-start(f32[1,1,256]{2,1,0:T(1,128)} %copy-done.7) | copy-start | bytes 3076
  100.3 22.0 %copy-start.10 = (f32[1,1,256]{2,1,0:T(1,128)S(1)}, f32[1,1,256]{2,1,0:T(1,128)}, u32[]{:S(2)}) copy-start(f32[1,1,256]{2,1,0:T(1,128)} %copy-done.9) | copy-start | bytes 3076
  100.4 22.0 %copy-start.12 = (f32[1,1,256]{2,1,0:T(1,128)S(1)}, f32[1,1,256]{2,1,0:T(1,128)}, u32[]{:S(2)}) copy-start(f32[1,1,256]{2,1,0:T(1,128)} %copy-done.11) | copy-start | bytes 3076
  100.4 22.0 %copy-start.14 = (f32[1,1,256]{2,1,0:T(1,128)S(1)}, f32[1,1,256]{2,1,0:T(1,128)}, u32[]{:S(2)}) copy-start(f32[1,1,256]{2,1,0:T(1,128)} %copy-done.13) | copy-start | bytes 3076
  100.4 22.0 %copy-start.16 = (f32[1,1,256]{2,1,0:T(1,128)S(1)}, f32[1,1,256]{2,1,0:T(1,128)}, u32[]{:S(2)}) copy-start(f32[1,1,256]{2,1,0:T(1,128)} %copy-done.15) | copy-start | bytes 3076
  100.4 22.0 %copy-start.18 = (f32[1,1,256]{2,1,0:T(1,128)S(1)}, f32[1,1,256]{2,1,0:T(1,128)}, u32[]{:S(2)}) copy-start(f32[1,1,256]{2,1,0:T(1,128)} %copy-done.17) | copy-start | bytes 3076
  100.4 22.0 %copy-start.20 = (f32[1,1,256]{2,1,0:T(1,128)S(1)}, f32[1,1,256]{2,1,0:T(1,128)}, u32[]{:S(2)}) copy-start(f32[1,1,256]{2,1,0:T(1,128)} %copy-done.19) | copy-start | bytes 3076
  100.4 22.0 %copy-start.22 = (f32[1,1,256]{2,1,0:T(1,128)S(1)}, f32[1,1,256]{2,1,0:T(1,128)}, u32[]{:S(2)}) copy-start(f32[1,1,256]{2,1,0:T(1,128)} %copy-done.21) | copy-start | bytes 3076
  100.4 22.0 %copy-start.24 = (f32[1,1,256]{2,1,0:T(1,128)S(1)}, f32[1,1,256]{2,1,0:T(1,128)}, u32[]{:S(2)}) copy-start(f32[1,1,256]{2,1,0:T(1,128)} %copy-done.23) | copy-start | bytes 3076
  100.4 22.0 %copy-start.26 = (f32[1,1,256]{2,1,0:T(1,128)S(1)}, f32[1,1,256]{2,1,0:T(1,128)}, u32[]{:S(2)}) copy-start(f32[1,1,256]{2,1,0:T(1,128)} %copy-done.25) | copy-start | bytes 3076
  100.4 22.0 %copy-start.28 = (f32[1,1,256]{2,1,0:T(1,128)S(1)}, f32[1,1,256]{2,1,0:T(1,128)}, u32[]{:S(2)}) copy-start(f32[1,1,256]{2,1,0:T(1,128)} %copy-done.27) | copy-start | bytes 3076
  100.4 22.0 %copy-start.30 = (f32[1,1,256]{2,1,0:T(1,128)S(1)}, f32[1,1,256]{2,1,0:T(1,128)}, u32[]{:S(2)}) copy-start(f32[1,1,256]{2,1,0:T(1,128)} %copy-done.29) | copy-start | bytes 3076
  100.5 22.0 %copy-start.32 = (f32[1,1,256]{2,1,0:T(1,128)S(1)}, f32[1,1,256]{2,1,0:T(1,128)}, u32[]{:S(2)}) copy-start(f32[1,1,256]{2,1,0:T(1,128)} %copy-done.31) | copy-start | bytes 3076
  100.5 22.0 %copy-start.34 = (f32[1,1,256]{2,1,0:T(1,128)S(1)}, f32[1,1,256]{2,1,0:T(1,128)}, u32[]{:S(2)}) copy-start(f32[1,1,256]{2,1,0:T(1,128)} %copy-done.33) | copy-start | bytes 3076
  100.5 22.0 %copy-start.36 = (f32[1,1,256]{2,1,0:T(1,128)S(1)}, f32[1,1,256]{2,1,0:T(1,128)}, u32[]{:S(2)}) copy-start(f32[1,1,256]{2,1,0:T(1,128)} %copy-done.35) | copy-start | bytes 3076
  100.5 22.0 %copy-start.38 = (f32[1,1,256]{2,1,0:T(1,128)S(1)}, f32[1,1,256]{2,1,0:T(1,128)}, u32[]{:S(2)}) copy-start(f32[1,1,256]{2,1,0:T(1,128)} %copy-done.37) | copy-start | bytes 3076
  100.5 22.0 %copy-start.40 = (f32[1,1,256]{2,1,0:T(1,128)S(1)}, f32[1,1,256]{2,1,0:T(1,128)}, u32[]{:S(2)}) copy-start(f32[1,1,256]{2,1,0:T(1,128)} %copy-done.39) | copy-start | bytes 3076
  100.5 22.0 %copy-start.42 = (f32[1,1,256]{2,1,0:T(1,128)S(1)}, f32[1,1,256]{2,1,0:T(1,128)}, u32[]{:S(2)}) copy-start(f32[1,1,256]{2,1,0:T(1,128)} %copy-done.41) | copy-start | bytes 3076
  100.5 22.0 %copy-start.44 = (f32[1,1,256]{2,1,0:T(1,128)S(1)}, f32[1,1,256]{2,1,0:T(1,128)}, u32[]{:S(2)}) copy-start(f32[1,1,256]{2,1,0:T(1,128)} %copy-done.43) | copy-start | bytes 3076
  100.5 22.0 %copy-start.46 = (f32[1,1,256]{2,1,0:T(1,128)S(1)}, f32[1,1,256]{2,1,0:T(1,128)}, u32[]{:S(2)}) copy-start(f32[1,1,256]{2,1,0:T(1,128)} %copy-done.45) | copy-start | bytes 3076
  100.5 22.0 %copy-start.48 = (f32[1,1,256]{2,1,0:T(1,128)S(1)}, f32[1,1,256]{2,1,0:T(1,128)}, u32[]{:S(2)}) copy-start(f32[1,1,256]{2,1,0:T(1,128)} %copy-done.47) | copy-start | bytes 3076
  100.5 22.0 %copy-start.50 = (f32[1,1,256]{2,1,0:T(1,128)S(1)}, f32[1,1,256]{2,1,0:T(1,128)}, u32[]{:S(2)}) copy-start(f32[1,1,256]{2,1,0:T(1,128)} %copy-done.49) | copy-start | bytes 3076
  100.6 22.0 %copy-start.52 = (f32[1,1,256]{2,1,0:T(1,128)S(1)}, f32[1,1,256]{2,1,0:T(1,128)}, u32[]{:S(2)}) copy-start(f32[1,1,256]{2,1,0:T(1,128)} %copy-done.51) | copy-start | bytes 3076
  100.6 22.0 %copy-start.54 = (f32[1,1,256]{2,1,0:T(1,128)S(1)}, f32[1,1,256]{2,1,0:T(1,128)}, u32[]{:S(2)}) copy-start(f32[1,1,256]{2,1,0:T(1,128)} %copy-done.53) | copy-start | bytes 3076
  100.6 22.0 %copy-start.56 = (f32[1,1,256]{2,1,0:T(1,128)S(1)}, f32[1,1,256]{2,1,0:T(1,128)}, u32[]{:S(2)}) copy-start(f32[1,1,256]{2,1,0:T(1,128)} %copy-done.55) | copy-start | bytes 3076
  100.6 22.0 %copy-start.58 = (f32[1,1,256]{2,1,0:T(1,128)S(1)}, f32[1,1,256]{2,1,0:T(1,128)}, u32[]{:S(2)}) copy-start(f32[1,1,256]{2,1,0:T(1,128)} %copy-done.57) | copy-start | bytes 3076
  100.6 22.0 %copy-start.60 = (f32[1,1,256]{2,1,0:T(1,128)S(1)}, f32[1,1,256]{2,1,0:T(1,128)}, u32[]{:S(2)}) copy-start(f32[1,1,256]{2,1,0:T(1,128)} %copy-done.59) | copy-start | bytes 3076
  100.6 22.0 %copy-start.62 = (f32[1,1,256]{2,1,0:T(1,128)S(1)}, f32[1,1,256]{2,1,0:T(1,128)}, u32[]{:S(2)}) copy-start(f32[1,1,256]{2,1,0:T(1,128)} %copy-done.61) | copy-start | bytes 3076
  100.6 22.0 %copy-start.64 = (f32[1,1,256]{2,1,0:T(1,128)S(1)}, f32[1,1,256]{2,1,0:T(1,128)}, u32[]{:S(2)}) copy-start(f32[1,1,256]{2,1,0:T(1,128)} %copy-done.63) | copy-start | bytes 3076
  100.6 22.0 %copy-start.66 = (f32[1,1,256]{2,1,0:T(1,128)S(1)}, f32[1,1,256]{2,1,0:T(1,128)}, u32[]{:S(2)}) copy-start(f32[1,1,256]{2,1,0:T(1,128)} %copy-done.65) | copy-start | bytes 3076
  100.6 22.0 %copy-start.68 = (f32[1,1,256]{2,1,0:T(1,128)S(1)}, f32[1,1,256]{2,1,0:T(1,128)}, u32[]{:S(2)}) copy-start(f32[1,1,256]{2,1,0:T(1,128)} %copy-done.67) | copy-start | bytes 3076
  100.6 22.0 %copy-start.70 = (f32[1,1,256]{2,1,0:T(1,128)S(1)}, f32[1,1,256]{2,1,0:T(1,128)}, u32[]{:S(2)}) copy-start(f32[1,1,256]{2,1,0:T(1,128)} %copy-done.69) | copy-start | bytes 3076
  100.7 22.0 %copy-start.72 = (f32[1,1,256]{2,1,0:T(1,128)S(1)}, f32[1,1,256]{2,1,0:T(1,128)}, u32[]{:S(2)}) copy-start(f32[1,1,256]{2,1,0:T(1,128)} %copy-done.71) | copy-start | bytes 3076
  100.7 22.0 %copy-start.74 = (f32[1,1,256]{2,1,0:T(1,128)S(1)}, f32[1,1,256]{2,1,0:T(1,128)}, u32[]{:S(2)}) copy-start(f32[1,1,256]{2,1,0:T(1,128)} %copy-done.73) | copy-start | bytes 3076
  117.8 33.6 %all-to-all-start.1 = ((bf16[16,68,256]{2,1,0:T(8,128)(2,1)}), bf16[16,68,256]{2,1,0:T(8,128)(2,1)S(1)}, u32[]{:S(2)}, u32[]{:S(2)}) async-start(bf16[16,68,256]{2,1,0:T(8,128)(2,1)} %broadcast_in_dim.43), calls=%async_computation.1 | async-start | bytes 1179648 | tf_op jit(solution)/shard_map/all_to_all | solution.py:149
  133.9 7.2 %collective-permute-start.4 = (bf16[1,3,54,256]{3,2,1,0:T(8,128)(2,1)S(1)}, bf16[1,3,54,256]{3,2,1,0:T(8,128)(2,1)S(1)}, u32[]{:S(2)}, u32[]{:S(2)}) collective-permute-start(bf16[1,3,54,256]{3,2,1,0:T(8,128)(2,1)S(1)} %fusion.244), channel_id=1, source_target_pairs={{0,16},{16,0},{2,18},{18,2},{4,20},{20,4},{6,22},{22,6},{8,24},{24... | collective-permute-start | bytes 248840 | tf_op jit(solution)/shard_map/ppermute | solution.py:27
  142.6 8.8 %collective-permute-start.5 = (bf16[2,1,16,3,256]{4,3,2,1,0:T(4,128)(2,1)S(1)}, bf16[2,1,16,3,256]{4,3,2,1,0:T(4,128)(2,1)S(1)}, u32[]{:S(2)}, u32[]{:S(2)}) collective-permute-start(bf16[2,1,16,3,256]{4,3,2,1,0:T(4,128)(2,1)S(1)} %pad_maximum_fusion.4), channel_id=1, source_target_pairs={{0,16},{16,0},{2,18},{18,2},{4,20},{20,4},{6,22},{22,6},{8,24},{24... | collective-permute-start | bytes 147464 | tf_op jit(solution)/shard_map/ppermute | solution.py:27
  143.9 9.0 %collective-permute-start.7 = (bf16[1,16,3,256]{3,2,1,0:T(4,128)(2,1)}, bf16[1,16,3,256]{3,2,1,0:T(4,128)(2,1)S(1)}, u32[]{:S(2)}, u32[]{:S(2)}) collective-permute-start(bf16[1,16,3,256]{3,2,1,0:T(4,128)(2,1)} %get-tuple-element.117), channel_id=1, source_target_pairs={{2,0},{4,2},{6,4},{8,6},{10,8},{12,10},{14,12},{16,14},{18,16},{20... | collective-permute-start | bytes 73736 | tf_op jit(solution)/shard_map/ppermute | solution.py:17
  145.2 7.7 %collective-permute-start.6 = (bf16[1,16,3,256]{3,2,1,0:T(4,128)(2,1)}, bf16[1,16,3,256]{3,2,1,0:T(4,128)(2,1)}, u32[]{:S(2)}, u32[]{:S(2)}) collective-permute-start(bf16[1,16,3,256]{3,2,1,0:T(4,128)(2,1)} %get-tuple-element.118), channel_id=1, source_target_pairs={{0,2},{2,4},{4,6},{6,8},{8,10},{10,12},{12,14},{14,16},{16,18},{18... | collective-permute-start | bytes 73736 | tf_op jit(solution)/shard_map/ppermute | solution.py:17
  152.3 6.0 %collective-permute-start.9 = (bf16[16,68,256]{2,0,1:T(8,128)(2,1)}, bf16[16,68,256]{2,0,1:T(8,128)(2,1)S(1)}, u32[]{:S(2)}, u32[]{:S(2)}) collective-permute-start(bf16[16,68,256]{2,0,1:T(8,128)(2,1)} %copy.50), channel_id=1, source_target_pairs={{0,2},{2,0},{1,3},{3,1},{4,6},{6,4},{5,7},{7,5},{8,10},{10,8},{9,1... | collective-permute-start | bytes 1671176 | tf_op jit(solution)/shard_map/ppermute | solution.py:168
  (50 other events, 749.1 us)
